TPU v7x, 512 devices: a whole 4x4x16 slice. The times are simulated.
512 devices in a mesh: lag: 64 (over z, x_hi, core), out: 8 (over x_lo, y).
Axes of the slice: x: 4 (x_hi: 2, x_lo: 2; x = x_hi * 2 + x_lo), y: 4, z: 16, core: 2. Of those that a mesh axis runs over, the one named last changes fastest.
Arguments:
- markov: float32 [2048, 256, 64], P('lag', 'out'), may hold values from -6 to 6
- basis: float32 [2048, 512], P('lag'), may hold values from -0.125 to 0.125
Outputs:
- reduced: float32 [64, 2, 512, 512], P('lag', None, 'out')
All inputs are finite; a program needn't handle non-finite values.
Results may differ from a plain program's by a relative error of at most 0.0003.
Values sent between devices are 32-bit elements; how exact they have to be, the bound alone decides.
A program may use at most 128 MiB of HBM per device.

v0:
```python
import jax
import jax.numpy as jnp
from jax import lax
from jax.sharding import PartitionSpec as P

P_SIZE = 256
S = 32
LAG_DEV = 32


def passed_along(block, axis, distance):
    devices = range(lax.axis_size(axis))
    route = [(i - distance, i) for i in devices if i - distance in devices]
    return lax.ppermute(block, axis, route)


def prefix(value, axis, join, neutral):
    count, mine = (lax.axis_size(axis), lax.axis_index(axis))
    pieces = lax.all_gather(value, axis)
    so_far = jnp.full_like(value, 0) + jnp.asarray(neutral, value.dtype)

    def step(position, so_far):
        longer = join(so_far, pieces[position])
        return jnp.where(position < mine, longer, so_far)

    return lax.fori_loop(0, count - 1, step, so_far)


def add_terms(earlier, later):
    return earlier + later


def body(markov, basis):
    lag_rows = markov.shape[0]
    out_rows = markov.shape[1]
    inputs = markov.shape[2]
    depth = S
    next_rows = passed_along(markov, "lag", -1)
    extended = jnp.concatenate([markov, next_rows], axis=0)
    slabs = [extended[j : j + lag_rows + 1] for j in range(depth)]
    hankel = jnp.stack(slabs, axis=2).reshape((lag_rows + 1) * out_rows, depth * inputs)
    width = basis.shape[1]
    projected = jnp.dot(
        hankel,
        lax.all_gather(basis, "lag", axis=0, tiled=True),
        preferred_element_type=jnp.float32,
        precision=lax.Precision.HIGHEST,
    )
    early = projected[: lag_rows * out_rows]
    later = projected[out_rows:]
    dims = (((0,), (0,)), ((), ()))
    first = lax.dot_general(early, early, dims, precision=lax.Precision.HIGHEST)
    second = lax.dot_general(early, later, dims, precision=lax.Precision.HIGHEST)
    grams = jnp.stack([first, second])
    share = width // lax.axis_size("out")
    summed = lax.psum(grams, "out")
    shared = lax.dynamic_slice_in_dim(summed, lax.axis_index("out") * share, share, 1)
    before = prefix(shared, "lag", add_terms, jnp.zeros_like(shared))
    total = before + shared
    counted = ((lax.axis_index("lag") + 1) * (LAG_DEV * P_SIZE)).astype(jnp.float32)
    return (total / counted)[None]


def solution(mesh):
    placed = (P("lag", "out", None), P("lag", None))
    return jax.shard_map(
        body, mesh=mesh, in_specs=placed, out_specs=P("lag", None, "out", None), check_vma=False
    )
```

profile of v0, /device:TPU:1, one launch (start us, length us, event | category | flops | bytes accessed | tf_op | source)
XLA Modules:
  0.0 559.5 jit_solution(16611541512673473530)
XLA Ops:
  6.5 8.8 %collective-permute-start = (f32[32,32,64]{2,1,0:T(8,128)}, f32[32,32,64]{2,1,0:T(8,128)S(1)}, u32[]{:S(2)}, u32[]{:S(2)}) collective-permute-start(f32[32,32,64]{2,1,0:T(8,128)} %param.4), channel_id=1, source_target_pairs={{8,0},{16,8},{24,16},{32,24},{40,32},{48,40},{56,48},{64,56},{72,6... | collective-permute-start | bytes 786440 | tf_op jit(solution)/shard_map/ppermute | solution.py:14
  15.4 1.1 constant_dynamic-update-slice_fusion.1
  16.5 3.2 collective-permute-done
  21.1 20.1 %copy.4 = f32[33,32,32,64]{3,2,1,0:T(8,128)} copy(f32[33,32,32,64]{3,1,0,2:T(8,128)S(1)} %fusion.13) | data formatting | bytes 17301504 | tf_op jit(solution)/shard_map/stack | solution.py:41
  41.2 15.1 %reshape.3 = f32[1056,2048]{1,0:T(8,128)} reshape(f32[33,32,32,64]{3,2,1,0:T(8,128)} %copy.4) | data formatting | bytes 17301504 | tf_op jit(solution)/shard_map/reshape | solution.py:41
  56.3 111.1 %all-gather.4.cloned.1.call-done = f32[2048,512]{1,0:T(8,128)} async-done(((f32[32,512]{1,0:T(8,128)}), f32[2048,512]{1,0:T(8,128)}) %all-gather.4.cloned.1.call-update) | async-done | bytes 4194320 | tf_op jit(solution)/shard_map/all_gather | solution.py:45
  167.4 17.1 %fusion.45 = f32[1056,512]{1,0:T(8,128)S(1)} fusion(f32[1056,2048]{1,0:T(8,128)} %reshape.3, f32[2048,512]{1,0:T(8,128)} %all-gather.4.cloned.1.call-done), kind=kOutput, calls=%fused_computation.77 | convolution fusion | flops 13287555072 | bytes 15007744 | tf_op jit(solution)/shard_map/dot_general | solution.py:43
  184.5 3.7 fusion.5
  188.2 3.6 fusion.8
  191.8 1.5 pad_maximum_fusion
  193.4 87.8 %all-reduce.2.cloned.1.call-done = f32[2,512,512]{2,1,0:T(8,128)} async-done(((f32[2,512,512]{2,1,0:T(8,128)}), f32[2,512,512]{2,1,0:T(8,128)}) %all-reduce.2.cloned.1.call-update) | async-done | bytes 2097168 | tf_op jit(solution)/shard_map/psum | solution.py:56
  281.2 1.7 constant_dynamic-slice_fusion
  282.9 200.7 %all-gather.6.cloned.1.call-done = f32[128,64,512]{2,1,0:T(8,128)} async-done(((f32[2,64,512]{2,1,0:T(8,128)}), f32[128,64,512]{2,1,0:T(8,128)}) %all-gather.6.cloned.1.call-update) | async-done | bytes 16777232 | tf_op jit(solution)/shard_map/all_gather | solution.py:19
  483.7 67.6 %while.14 = (s32[]{:T(128)}, f32[2,64,512]{2,1,0:T(8,128)S(1)}, s32[]{:T(128)}, f32[64,2,64,512]{3,2,1,0:T(8,128)}, s32[]{:T(128)}, /*index=5*/s32[]{:T(128)}) while((s32[]{:T(128)}, f32[2,64,512]{2,1,0:T(8,128)S(1)}, s32[]{:T(128)}, f32[64,2,64,512]{3,2,1,0:T(8,128)}, s32[]{:T(128)}, /*index=5*/s32[]{:T(128)}) %tuple.41), condition=%wide.region_2.3_spmd.clone, body=%wide.region_1.2_spmd.clone.sunk | while | flops 196612 | bytes 786525 | solution.py:26
  486.9 1.0 add_select_fusion.2
  488.0 1.0 add_select_fusion.2
  489.0 1.0 add_select_fusion.2
  491.2 1.0 add_select_fusion.2
  492.2 1.0 add_select_fusion.2
  493.3 1.0 add_select_fusion.2
  494.4 1.0 add_select_fusion.2
  496.5 1.0 add_select_fusion.2
  497.6 1.0 add_select_fusion.2
  498.7 1.0 add_select_fusion.2
  501.9 1.0 add_select_fusion.2
  503.0 1.0 add_select_fusion.2
  504.1 1.0 add_select_fusion.2
  507.3 1.0 add_select_fusion.2
  508.4 1.0 add_select_fusion.2
  509.4 1.0 add_select_fusion.2
  511.6 1.0 add_select_fusion.2
  551.3 1.7 divide_bitcast_fusion
  (86 shorter events, 49.7 us)
Async XLA Ops:
  6.5 160.9 %all-gather.4.cloned.1.call-start = ((), (), s32[]{:S(2)}) async-start(), calls=%async_computation | async-start | bytes 4259840 | tf_op jit(solution)/shard_map/all_gather | solution.py:45
  6.5 13.1 %collective-permute-start = (f32[32,32,64]{2,1,0:T(8,128)}, f32[32,32,64]{2,1,0:T(8,128)S(1)}, u32[]{:S(2)}, u32[]{:S(2)}) collective-permute-start(f32[32,32,64]{2,1,0:T(8,128)} %param.4), channel_id=1, source_target_pairs={{8,0},{16,8},{24,16},{32,24},{40,32},{48,40},{56,48},{64,56},{72,6... | collective-permute-start | bytes 786440 | tf_op jit(solution)/shard_map/ppermute | solution.py:14
  15.3 265.9 %all-reduce.2.cloned.1.call-start = ((), (), s32[]{:S(2)}) async-start(), calls=%async_computation.1 | async-start | bytes 4194304 | tf_op jit(solution)/shard_map/psum | solution.py:56
  193.4 290.3 %all-gather.6.cloned.1.call-start = ((), (), s32[]{:S(2)}) async-start(), calls=%async_computation.2 | async-start | bytes 17039360 | tf_op jit(solution)/shard_map/all_gather | solution.py:19
Sparse Core Ops, SparseCore 0:
  15.5 151.9 all-gather.3
  193.5 87.7 all-reduce.1
  284.5 199.0 all-gather.5
where the time goes:
time: 562 us; the launch traced here: 560 us
  waiting for transfers between devices  403 us (72%)
  other arithmetic  69.3 us (12%)
  local copies, waits for them, and re-layouts  39.2 us (7%)
  matrix products  24.4 us (4%)
  between operations  13.4 us (2%)
  starting transfers between devices  8.86 us (2%)
    all_gather x1, waiting for transfers between devices, prefix(): pieces = lax.all_gather(value, axis)  201 us
    all_gather x1, waiting for transfers between devices, body(): lax.all_gather(basis, 'lag', axis=0, tiled=True)  111 us
    psum x1, waiting for transfers between devices, body(): summed = lax.psum(grams, 'out')  87.8 us
    select_n x63, other arithmetic, step(): return jnp.where(position < mine, longer, so_far)  66.1 us
    another operation x2, local copies, waits for them, and re-layouts, body(): jnp.stack(slabs, axis=2).reshape((lag_rows + 1) * out_rows, depth * inputs)  20.1 us
    dot_general x1, matrix products, body(): jnp.dot(hankel, lax.all_gather(basis, 'lag', axis=0, tiled=True), preferr...  17.1 us
    reshape x1, local copies, waits for them, and re-layouts, body(): jnp.stack(slabs, axis=2).reshape((lag_rows + 1) * out_rows, depth * inputs)  15.1 us
  transfers between devices with their start and end apart: 4, of which 4 were waited for; matrix products, arithmetic and copies ran while one was open for 7% of the time, Pallas kernels for 0%

commit v1 on v0

v1 whole, which is shorter than its diff:
```python
import jax
import jax.numpy as jnp
from jax import lax
from jax.experimental import pallas as pl
from jax.experimental.pallas import tpu as pltpu
from jax.sharding import PartitionSpec as P

P_SIZE = 256
LAG_DEV = 32
MESH = pl.DeviceIdType.MESH
F32 = jnp.float32
BF16 = jnp.bfloat16

NZ = 16
CHUNKS = 4
ROWS = 1056
TILE_M = 528


def split(value):
    high = value.astype(BF16)
    low = (value - high.astype(F32)).astype(BF16)
    return high, low


def device(x, y, z, core):
    return (4 * z + 2 * lax.div(x, 2) + core, 4 * lax.rem(x, 2) + y)


def dot(a, b):
    return jnp.dot(a, b, preferred_element_type=F32)


def kernel(
    markov, basis, out,
    packed, pairs, lhs, gathered, weights, proj, right_hi, right_lo, left_hi, left_lo,
    gram_out, gram_in, gram, plane, states, tiles_out, tiles_in, before_out, before_in, final,
    mk_s, mk_r, b1_s, b1_r, b2_s, b2_r, b3_s, b3_r, b4_s, b4_r, cs_s, cs_r, pl_s, pl_r,
    e1_s, e1_r, e2_s, e2_r, f_s, f_r,
):
    lag = lax.axis_index("lag")
    chan = lax.axis_index("out")
    z = lax.div(lag, 4)
    x_hi = lax.rem(lax.div(lag, 2), 2)
    core = lax.rem(lag, 2)
    x_lo = lax.div(chan, 4)
    y = lax.rem(chan, 4)
    x = 2 * x_hi + x_lo
    block = 4 * z + x
    swapped = core != x_lo

    def remote(src, dst, send, recv, to):
        return pltpu.make_async_remote_copy(
            src_ref=src, dst_ref=dst, send_sem=send, recv_sem=recv, device_id=to, device_id_type=MESH
        )

    def around(value, step, size):
        return lax.rem(value + step, size)

    barrier = pltpu.get_barrier_semaphore()

    def greet(to):
        pl.semaphore_signal(barrier, inc=1, device_id=to, device_id_type=MESH)

    @pl.loop(1, NZ)
    def _(d):
        greet(device(x, y, around(z, d, NZ), core))

    @pl.loop(1, 16)
    def _(d):
        greet(device(around(x, lax.div(d, 4), 4), around(y, lax.rem(d, 4), 4), z, core))

    @pl.loop(0, 4)
    def _(d):
        greet(device(around(x, d, 4), y, z, 1 - core))

    gives_down = jnp.logical_and(lax.rem(lag, 4) == 0, z > 0)
    takes_up = jnp.logical_and(x == 3, z < NZ - 1)

    @pl.when(gives_down)
    def _():
        greet(device(3, y, z - 1, x_lo))

    @pl.when(takes_up)
    def _():
        greet((4 * (z + 1), 4 * core + y))

    for t in range(LAG_DEV // 2):
        packed[t] = jnp.concatenate([markov[2 * t], markov[2 * t + 1]], axis=-1)

    rows8 = pl.ds(pl.multiple_of(8 * y, 8), 8)
    cols = pl.ds(pl.multiple_of(256 * x_lo, 256), 256)
    gathered[z, x_hi, core, y, :, cols] = basis[rows8, cols]

    pl.semaphore_wait(barrier, 34 + gives_down.astype(jnp.int32) + takes_up.astype(jnp.int32))

    def level1(d, zz):
        piece = gathered.at[zz, x_hi, core, y, :, cols]
        return remote(piece, piece, b1_s.at[d - 1], b1_r.at[d - 1], device(x, y, around(z, d, NZ), core))

    @pl.loop(1, NZ)
    def _(d):
        level1(d, z).start()

    def to_block():
        return remote(packed, pairs.at[0], mk_s.at[0], mk_r.at[0], device(2 * x_hi + core, y, z, x_lo))

    def to_before():
        earlier = lag - 1
        to = device(lax.rem(earlier, 4), y, lax.div(earlier, 4), x_lo)
        return remote(packed, pairs.at[1], mk_s.at[1], mk_r.at[1], to)

    @pl.when(swapped)
    def _():
        to_block().start()

    @pl.when(lag > 0)
    def _():
        to_before().start()

    @pl.when(jnp.logical_not(swapped))
    def _():
        pairs[0] = packed[...]

    @pl.when(block == 4 * NZ - 1)
    def _():
        pairs[1] = jnp.zeros_like(packed)

    def chunk_of(q):
        return lax.rem(lax.div(z, 4) + q, CHUNKS)

    def zs_of(q):
        return pl.ds(4 * chunk_of(q), 4)

    def wait_level1(q):
        @pl.loop(0, 4)
        def _(i):
            source = 4 * chunk_of(q) + i
            d = lax.rem(z - source + NZ, NZ)

            @pl.when(d > 0)
            def _():
                level1(d, source).wait_recv()

    def level2(q, d):
        piece = gathered.at[zs_of(q), x_hi, core, y, :, cols]
        along_y = core == 0
        to = device(
            jnp.where(along_y, x, around(x, d, 4)), jnp.where(along_y, around(y, d, 4), y), z, core
        )
        slot = 3 * q + d - 1
        return remote(piece, piece, b2_s.at[slot], b2_r.at[slot], to)

    def level3(q, d, which):
        slot = 3 * q + d - 1
        if which == 0:
            piece = gathered.at[zs_of(q), x_hi, 0, :, :, cols]
            to = device(around(x, d, 4), y, z, 0)
        else:
            piece = gathered.at[zs_of(q), :, 1, y]
            to = device(x, around(y, d, 4), z, 1)
        return remote(piece, piece, b3_s.at[slot], b3_r.at[slot], to)

    def by_core(act):
        for which in (0, 1):
            @pl.when(core == which)
            def _():
                act(which)

    def level4(q):
        piece = gathered.at[zs_of(q), :, core]
        return remote(piece, piece, b4_s.at[q], b4_r.at[q], device(x, y, z, 1 - core))

    def wait2_start3(q):
        for d in (1, 2, 3):
            level2(q, d).wait_recv()

        def act(which):
            for d in (1, 2, 3):
                level3(q, d, which).start()

        by_core(act)

    def wait3_start4(q):
        def act(which):
            for d in (1, 2, 3):
                level3(q, d, which).wait_recv()

        by_core(act)
        level4(q).start()

    def wait1_start2(q):
        wait_level1(q)
        for d in (1, 2, 3):
            level2(q, d).start()

    def build_lhs():
        @pl.when(swapped)
        def _():
            to_block().wait_recv()

        @pl.when(block < 4 * NZ - 1)
        def _():
            to_before().wait_recv()

        first_half = lax.broadcasted_iota(jnp.int32, (32, 128), 1) < 64

        def put(t, value):
            high, low = split(value)
            for place, part in ((0, high), (256, low), (512, high)):
                lhs[pl.ds(pl.multiple_of(32 * t + 64, 32), 32), place : place + 128] = part
                lhs[pl.ds(pl.multiple_of(32 * t, 32), 32), place + 128 : place + 256] = part

        def both(t, this, following):
            put(2 * t, this)
            put(2 * t + 1, jnp.where(first_half, pltpu.roll(this, 64, 1), pltpu.roll(following, 64, 1)))

        for side in (0, 1):
            @pl.loop(0, 15)
            def _(t):
                both(16 * side + t, pairs[side, t], pairs[side, t + 1])

        both(15, pairs[0, 15], pairs[1, 0])
        put(62, pairs[1, 15])

    def compute(q):
        level4(q).wait_recv()

        @pl.loop(0, 2)
        def _(k):
            part = 2 * chunk_of(q) + k
            for i in range(2):
                for h in range(2):
                    for w in range(2):
                        high, low = split(gathered[2 * part + i, h, w].reshape(32, 512))
                        at = 128 * i + 64 * h + 32 * w
                        weights[at : at + 32, :] = high
                        weights[256 + at : 288 + at, :] = high
                        weights[512 + at : 544 + at, :] = low

            @pl.loop(0, ROWS // TILE_M)
            def _(m):
                here = pl.ds(pl.multiple_of(TILE_M * m, 16), TILE_M)
                there = pl.ds(pl.multiple_of(128 * part + 64 + TILE_M * m, 16), TILE_M)
                proj[here, :] += dot(lhs[there, :], weights[...])

    wait1_start2(0)
    build_lhs()
    proj[...] = jnp.zeros_like(proj)
    for step in range(1, CHUNKS + 3):
        if 0 <= step - 1 < CHUNKS:
            wait2_start3(step - 1)
        if 0 <= step - 2 < CHUNKS:
            wait3_start4(step - 2)
        if step < CHUNKS:
            wait1_start2(step)
        if 0 <= step - 3 < CHUNKS:
            compute(step - 3)

    @pl.loop(0, 8)
    def _(i):
        here = pl.ds(pl.multiple_of(128 * i, 128), 128)
        value = proj[here, :]
        high, low = split(value)
        right_hi[here, :] = high
        right_lo[here, :] = low
        high, low = split(value.T)
        left_hi[:, here] = high
        left_lo[:, here] = low

    high, low = split(proj[1024:ROWS, :])
    right_hi[1024:ROWS, :] = high
    right_lo[1024:ROWS, :] = low

    def half_gram(half, g):
        rows = pl.ds(pl.multiple_of(256 * half, 256), 256)
        there = slice(32 * g, 32 * g + 1024)
        total = dot(left_hi[rows, :], right_hi[there, :])
        total += dot(left_lo[rows, :], right_hi[there, :])
        total += dot(left_hi[rows, :], right_lo[there, :])
        return total

    def core_sum(g):
        return remote(gram_out.at[g], gram_in.at[g], cs_s.at[g], cs_r.at[g], device(x, y, z, 1 - core))

    for g in (0, 1):
        gram_out[g] = half_gram(1 - core, g)
        core_sum(g).start()
    for g in (0, 1):
        gram[g] = half_gram(core, g)
    for g in (0, 1):
        core_sum(g).wait_recv()
        gram[g] += gram_in[g]

    def to_plane(d):
        tx = around(x, lax.div(d, 4), 4)
        ty = around(y, lax.rem(d, 4), 4)
        src = gram.at[:, pl.ds(pl.multiple_of(64 * ty + 16 * tx, 16), 16), :]
        return remote(src, plane.at[x, y], pl_s.at[d - 1], pl_r.at[d - 1], device(tx, ty, z, core))

    @pl.loop(1, 16)
    def _(d):
        to_plane(d).start()

    plane[x, y] = gram[:, pl.ds(pl.multiple_of(64 * y + 16 * x, 16), 16), :]

    @pl.loop(1, 16)
    def _(d):
        to_plane(d).wait_recv()

    state = None
    for i in range(4):
        term = (plane[i, 0] + plane[i, 1]) + (plane[i, 2] + plane[i, 3])
        state = term if state is None else state + term
        states[i] = state

    def tile(t):
        return (t // 8, slice(8 * (t // 4 % 2), 8 * (t // 4 % 2) + 8), slice(128 * (t % 4), 128 * (t % 4) + 128))

    for t in range(NZ):
        tiles_out[t] = states[(3,) + tile(t)]

    def scatter(d):
        to = around(z, d, NZ)
        return remote(tiles_out.at[to], tiles_in.at[z], e1_s.at[d - 1], e1_r.at[d - 1], device(x, y, to, core))

    def bring_back(d):
        to = around(z, d, NZ)
        return remote(before_out.at[to], before_in.at[z], e2_s.at[d - 1], e2_r.at[d - 1], device(x, y, to, core))

    @pl.loop(1, NZ)
    def _(d):
        scatter(d).start()

    tiles_in[z] = tiles_out[z]

    @pl.loop(1, NZ)
    def _(d):
        scatter(d).wait_recv()

    running = jnp.zeros((8, 128), F32)
    for t in range(NZ):
        before_out[t] = running
        running = running + tiles_in[t]

    @pl.loop(1, NZ)
    def _(d):
        bring_back(d).start()

    before_in[z] = before_out[z]

    @pl.loop(1, NZ)
    def _(d):
        bring_back(d).wait_recv()

    own_rows = pl.ds(pl.multiple_of(16 * x, 16), 16)

    def to_owner(i):
        to = device(2 * (i // 2) + core, y, z, i % 2)
        return remote(final.at[i], out.at[0, :, own_rows, :], f_s.at[i], f_r.at[x], to)

    def mine(i):
        return jnp.logical_and(x == 2 * (i // 2) + core, core == i % 2)

    for i in range(4):
        count = ((4 * z + i + 1) * (LAG_DEV * P_SIZE)).astype(F32)
        for t in range(NZ):
            final[(i,) + tile(t)] = (before_in[t] + states[(i,) + tile(t)]) / count

        @pl.when(mine(i))
        def _():
            out[0, :, own_rows, :] = final[i]

        @pl.when(jnp.logical_not(mine(i)))
        def _():
            to_owner(i).start()

    def from_source(i):
        rows = pl.ds(16 * i, 16)
        here = out.at[0, :, rows, :]
        return remote(final.at[0], here, f_s.at[0], f_r.at[i], device(x, y, z, 1 - core))

    for i in range(4):
        @pl.when(jnp.logical_not(jnp.logical_and(x == i, core == x_lo)))
        def _():
            from_source(i).wait_recv()

    @pl.loop(1, NZ)
    def _(d):
        level1(d, z).wait_send()
        to_plane(d).wait_send()
        scatter(d).wait_send()
        bring_back(d).wait_send()

    @pl.when(swapped)
    def _():
        to_block().wait_send()

    @pl.when(lag > 0)
    def _():
        to_before().wait_send()

    for q in range(CHUNKS):
        for d in (1, 2, 3):
            level2(q, d).wait_send()

        def act(which):
            for d in (1, 2, 3):
                level3(q, d, which).wait_send()

        by_core(act)
        level4(q).wait_send()
    for g in (0, 1):
        core_sum(g).wait_send()
    for i in range(4):
        @pl.when(jnp.logical_not(mine(i)))
        def _():
            to_owner(i).wait_send()


def body(markov, basis):
    vmem = pl.BlockSpec(memory_space=pltpu.VMEM)
    counts = [2, 2, 15, 15, 12, 12, 12, 12, 4, 4, 2, 2, 15, 15, 15, 15, 15, 15, 4, 4]
    return pl.pallas_call(
        kernel,
        out_shape=jax.ShapeDtypeStruct((1, 2, 64, 512), F32),
        in_specs=[vmem, vmem],
        out_specs=vmem,
        scratch_shapes=[
            pltpu.VMEM((16, 32, 128), F32),
            pltpu.VMEM((2, 16, 32, 128), F32),
            pltpu.VMEM((2080, 768), BF16),
            pltpu.VMEM((16, 2, 2, 4, 8, 512), F32),
            pltpu.VMEM((768, 512), BF16),
            pltpu.VMEM((ROWS, 512), F32),
            pltpu.VMEM((ROWS, 512), BF16),
            pltpu.VMEM((ROWS, 512), BF16),
            pltpu.VMEM((512, 1024), BF16),
            pltpu.VMEM((512, 1024), BF16),
            pltpu.VMEM((2, 256, 512), F32),
            pltpu.VMEM((2, 256, 512), F32),
            pltpu.VMEM((2, 256, 512), F32),
            pltpu.VMEM((4, 4, 2, 16, 512), F32),
            pltpu.VMEM((4, 2, 16, 512), F32),
            pltpu.VMEM((NZ, 8, 128), F32),
            pltpu.VMEM((NZ, 8, 128), F32),
            pltpu.VMEM((NZ, 8, 128), F32),
            pltpu.VMEM((NZ, 8, 128), F32),
            pltpu.VMEM((4, 2, 16, 512), F32),
        ]
        + [pltpu.SemaphoreType.DMA((n,)) for n in counts],
        compiler_params=pltpu.CompilerParams(
            collective_id=0, has_side_effects=True, vmem_limit_bytes=48 * 1024 * 1024
        ),
        cost_estimate=pl.CostEstimate(flops=10_000_000_000, bytes_accessed=1_000_000, transcendentals=0),
    )(markov, basis)


def solution(mesh):
    placed = (P("lag", "out", None), P("lag", None))
    return jax.shard_map(
        body, mesh=mesh, in_specs=placed, out_specs=P("lag", None, "out", None), check_vma=False
    )
```

time: 562 us -> 106 us (0.19)
  waiting for transfers between devices: 403 us -> 0 us
  Pallas kernels: 0 us -> 103 us
  other arithmetic: 69.3 us -> 0 us
  local copies, waits for them, and re-layouts: 39.2 us -> 2.59 us
  matrix products: 24.4 us -> 0 us
  between operations: 13.4 us -> 0.01 us
  starting transfers between devices: 8.86 us -> 0 us
    all_gather x2 -> x0, waiting for transfers between devices: 312 us -> none  [the longest x1 201 us: prefix(): pieces = lax.all_gather(value, axis)]
    pallas_call x0 -> x1, Pallas kernels: none -> 103 us  [body(): pl.pallas_call(kernel, out_shape=jax.ShapeDtypeStruct((1, 2, 64, 512), F3...]
    psum x1 -> x0, waiting for transfers between devices: 87.8 us -> none  [body(): summed = lax.psum(grams, 'out')]
    select_n x63 -> x0, other arithmetic: 66.1 us -> none  [step(): return jnp.where(position < mine, longer, so_far)]
    dot_general x3 -> x0, matrix products: 24.4 us -> none  [the longest x1 17.1 us: body(): jnp.dot(hankel, lax.all_gather(basis, 'lag', axis=0, tiled=True), preferr...]
    another operation x2 -> x0, local copies, waits for them, and re-layouts: 20.1 us -> none  [body(): jnp.stack(slabs, axis=2).reshape((lag_rows + 1) * out_rows, depth * inputs)]
    reshape x1 -> x0, local copies, waits for them, and re-layouts: 15.1 us -> none  [body(): jnp.stack(slabs, axis=2).reshape((lag_rows + 1) * out_rows, depth * inputs)]
    ppermute x1 -> x0, starting transfers between devices: 8.77 us -> none  [passed_along(): return lax.ppermute(block, axis, route)]
  transfers between devices with their start and end apart: 4 -> 0, of which waited for: 4 -> 0; matrix products, arithmetic and copies ran while one was open for 7% -> 0% of each run, Pallas kernels for 0% -> 0%
where the time goes in v1:
time: 106 us
  Pallas kernels  103 us (97%)
  local copies, waits for them, and re-layouts  2.59 us (2%)
    pallas_call x1, Pallas kernels, body(): pl.pallas_call(kernel, out_shape=jax.ShapeDtypeStruct((1, 2, 64, 512), F3...  103 us
    unnamed x5, local copies, waits for them, and re-layouts  2.59 us

profile of v1, /device:TPU:1, one launch (start us, length us, event | category | flops | bytes accessed | tf_op | source)
XLA Modules:
  0.0 106.1 jit_solution(1358391954642423090)
XLA Ops:
  0.0 0.0 copy-start
  0.0 1.0 copy-done
  1.0 0.0 copy-start.1
  1.0 0.8 copy-done.1
  1.9 103.5 %shard_map.28 = f32[1,2,64,512]{3,2,1,0:T(8,128)S(1)} custom-call(f32[32,32,64]{2,1,0:T(8,128)S(1)} %copy-done, f32[32,512]{1,0:T(8,128)S(1)} %copy-done.1), custom_call_target="tpu_custom_call" | custom-call | flops 10000000000 | bytes 1000000 | tf_op jit(solution)/shard_map/pallas_call | solution.py:424
  105.4 0.7 copy.4
Async XLA Ops:
  0.0 1.0 copy-start
  1.0 0.8 copy-start.1

commit v2 on v1

v2 whole, which is shorter than its diff:
```python
import functools

import jax
import jax.numpy as jnp
from jax import lax
from jax.experimental import pallas as pl
from jax.experimental.pallas import tpu as pltpu
from jax.sharding import PartitionSpec as P

P_SIZE = 256
LAG_DEV = 32
MESH = pl.DeviceIdType.MESH
F32 = jnp.float32
BF16 = jnp.bfloat16

NZ = 16
CHUNKS = 8
SECOND, THIRD, LAST = 3, 6, 7
ROWS = 1056
TILE_M = 528


def split(value):
    high = value.astype(BF16)
    low = (value - high.astype(F32)).astype(BF16)
    return high, low


def device(x, y, z, core):
    return (4 * z + 2 * lax.div(x, 2) + core, 4 * lax.rem(x, 2) + y)


def dot(a, b):
    return jnp.dot(a, b, preferred_element_type=F32)


def kernel(
    markov_hbm, basis, out,
    markov, packed, pairs, lhs, gathered, weights, proj, right_hi, right_lo, left_hi, left_lo,
    gram_out, gram_in, gram, plane, states, tiles_out, tiles_in, before_out, before_in, final,
    mk_s, mk_r, b1_s, b1_r, b2_s, b2_r, b3_s, b3_r, b4_s, b4_r, cs_s, cs_r, pl_s, pl_r,
    e1_s, e1_r, e2_s, e2_r, f_s, f_r, in_s,
):
    lag = lax.axis_index("lag")
    chan = lax.axis_index("out")
    z = lax.div(lag, 4)
    x_hi = lax.rem(lax.div(lag, 2), 2)
    core = lax.rem(lag, 2)
    x_lo = lax.div(chan, 4)
    y = lax.rem(chan, 4)
    x = 2 * x_hi + x_lo
    block = 4 * z + x
    swapped = core != x_lo

    def remote(src, dst, send, recv, to):
        return pltpu.make_async_remote_copy(
            src_ref=src, dst_ref=dst, send_sem=send, recv_sem=recv, device_id=to, device_id_type=MESH
        )

    def around(value, step, size):
        return lax.rem(value + step, size)

    rows8 = pl.ds(pl.multiple_of(8 * y, 8), 8)
    cols = pl.ds(pl.multiple_of(256 * x_lo, 256), 256)
    take_markov = pltpu.make_async_copy(markov_hbm, markov, in_s.at[0])
    take_basis = pltpu.make_async_copy(
        basis.at[rows8, cols], gathered.at[z, x_hi, core, y, :, cols], in_s.at[1]
    )
    take_markov.start()
    take_basis.start()

    drains = []

    def loop_drain(make, count):
        def act():
            @pl.loop(1, count)
            def _(d):
                make(d).wait_send()

        drains.append(act)

    def when_drain(condition, make):
        def act():
            @pl.when(condition)
            def _():
                make().wait_send()

        drains.append(act)

    barrier = pltpu.get_barrier_semaphore()

    def greet(to):
        pl.semaphore_signal(barrier, inc=1, device_id=to, device_id_type=MESH)

    @pl.loop(1, NZ)
    def _(d):
        greet(device(x, y, around(z, d, NZ), core))

    @pl.loop(1, 16)
    def _(d):
        greet(device(around(x, lax.div(d, 4), 4), around(y, lax.rem(d, 4), 4), z, core))

    @pl.loop(0, 4)
    def _(d):
        greet(device(around(x, d, 4), y, z, 1 - core))

    gives_down = jnp.logical_and(lax.rem(lag, 4) == 0, z > 0)
    takes_up = jnp.logical_and(x == 3, z < NZ - 1)

    @pl.when(gives_down)
    def _():
        greet(device(3, y, z - 1, x_lo))

    @pl.when(takes_up)
    def _():
        greet((4 * (z + 1), 4 * core + y))

    take_markov.wait()
    for t in range(LAG_DEV // 2):
        packed[t] = jnp.concatenate([markov[2 * t], markov[2 * t + 1]], axis=-1)

    take_basis.wait()
    pl.semaphore_wait(barrier, 34 + gives_down.astype(jnp.int32) + takes_up.astype(jnp.int32))


    def level1(d, zz):
        piece = gathered.at[zz, x_hi, core, y, :, cols]
        return remote(piece, piece, b1_s.at[d - 1], b1_r.at[d - 1], device(x, y, around(z, d, NZ), core))

    @pl.loop(0, NZ - 1)
    def _(k):
        near = lax.div(k, 2)
        level1(jnp.where(lax.rem(k, 2) == 0, near + 1, NZ - 1 - near), z).start()

    loop_drain(lambda d: level1(d, z), NZ)

    def to_block():
        return remote(packed, pairs.at[0], mk_s.at[0], mk_r.at[0], device(2 * x_hi + core, y, z, x_lo))

    def to_before():
        earlier = lag - 1
        to = device(lax.rem(earlier, 4), y, lax.div(earlier, 4), x_lo)
        return remote(packed, pairs.at[1], mk_s.at[1], mk_r.at[1], to)

    @pl.when(swapped)
    def _():
        to_block().start()

    @pl.when(lag > 0)
    def _():
        to_before().start()

    when_drain(swapped, to_block)
    when_drain(lag > 0, to_before)

    @pl.when(jnp.logical_not(swapped))
    def _():
        pairs[0] = packed[...]

    @pl.when(block == 4 * NZ - 1)
    def _():
        pairs[1] = jnp.zeros_like(packed)

    def chunk_of(q):
        away = (q + 1) // 2 if q % 2 else CHUNKS - q // 2
        return lax.rem(lax.div(z, 2) + away, CHUNKS)

    def zs_of(q):
        return pl.ds(2 * chunk_of(q), 2)

    def wait_level1(q):
        @pl.loop(0, 2)
        def _(i):
            source = 2 * chunk_of(q) + i
            d = lax.rem(z - source + NZ, NZ)

            @pl.when(d > 0)
            def _():
                level1(d, source).wait_recv()

    def level2(q, d):
        piece = gathered.at[zs_of(q), x_hi, core, y, :, cols]
        x_next, y_next = device(around(x, d, 4), y, z, core), device(x, around(y, d, 4), z, core)
        to = tuple(jnp.where(core == 0, b, a) for a, b in zip(x_next, y_next))
        slot = 3 * q + d - 1
        return remote(piece, piece, b2_s.at[slot], b2_r.at[slot], to)

    def level3(q, d, x_last):
        slot = 3 * q + d - 1
        if x_last:
            piece = gathered.at[zs_of(q), x_hi, core, :, :, cols]
            to = device(around(x, d, 4), y, z, core)
        else:
            piece = gathered.at[zs_of(q), :, core, y]
            to = device(x, around(y, d, 4), z, core)
        return remote(piece, piece, b3_s.at[slot], b3_r.at[slot], to)

    def by_order(act):
        for x_last in (True, False):
            @pl.when((core == 0) == x_last)
            def _():
                act(x_last)

    def level4(q):
        piece = gathered.at[zs_of(q), :, core]
        return remote(piece, piece, b4_s.at[q], b4_r.at[q], device(x, y, z, 1 - core))

    def wait2_start3(q):
        for d in (1, 2, 3):
            level2(q, d).wait_recv()

        def act(x_last):
            for d in (1, 2, 3):
                level3(q, d, x_last).start()

        def drain(x_last):
            for d in (1, 2, 3):
                level3(q, d, x_last).wait_send()

        by_order(act)
        drains.append(lambda: by_order(drain))

    def wait3_start4(q):
        def act(x_last):
            for d in (1, 2, 3):
                level3(q, d, x_last).wait_recv()

        by_order(act)
        level4(q).start()
        drains.append(lambda: level4(q).wait_send())

    def wait1_start2(q):
        wait_level1(q)
        for d in (1, 2, 3):
            level2(q, d).start()

        def drain():
            for d in (1, 2, 3):
                level2(q, d).wait_send()

        drains.append(drain)

    def build_lhs():
        @pl.when(swapped)
        def _():
            to_block().wait_recv()

        @pl.when(block < 4 * NZ - 1)
        def _():
            to_before().wait_recv()

        first_half = lax.broadcasted_iota(jnp.int32, (32, 128), 1) < 64

        def put(t, value):
            high, low = split(value)
            for place, part in ((0, high), (256, low), (512, high)):
                lhs[pl.ds(pl.multiple_of(32 * t + 64, 32), 32), place : place + 128] = part
                lhs[pl.ds(pl.multiple_of(32 * t, 32), 32), place + 128 : place + 256] = part

        def both(t, this, following):
            put(2 * t, this)
            put(2 * t + 1, jnp.where(first_half, pltpu.roll(this, 64, 1), pltpu.roll(following, 64, 1)))

        for side in (0, 1):
            @pl.loop(0, 15)
            def _(t):
                both(16 * side + t, pairs[side, t], pairs[side, t + 1])

        both(15, pairs[0, 15], pairs[1, 0])
        put(62, pairs[1, 15])

    def compute(q):
        level4(q).wait_recv()

        part = chunk_of(q)
        for i in range(2):
            for h in range(2):
                for w in range(2):
                    high, low = split(gathered[2 * part + i, h, w].reshape(32, 512))
                    at = 128 * i + 64 * h + 32 * w
                    weights[at : at + 32, :] = high
                    weights[256 + at : 288 + at, :] = high
                    weights[512 + at : 544 + at, :] = low

        @pl.loop(0, ROWS // TILE_M)
        def _(m):
            here = pl.ds(pl.multiple_of(TILE_M * m, 16), TILE_M)
            there = pl.ds(pl.multiple_of(128 * part + 64 + TILE_M * m, 16), TILE_M)
            proj[here, :] += dot(lhs[there, :], weights[...])


    proj[...] = jnp.zeros_like(proj)
    for step in range(CHUNKS + LAST):
        if step < CHUNKS:
            wait1_start2(step)
        if 0 <= step - SECOND < CHUNKS:
            wait2_start3(step - SECOND)
        if 0 <= step - THIRD < CHUNKS:
            wait3_start4(step - THIRD)
        if step == LAST:
            build_lhs()
        if 0 <= step - LAST < CHUNKS:
            compute(step - LAST)


    @pl.loop(0, 8)
    def _(i):
        here = pl.ds(pl.multiple_of(128 * i, 128), 128)
        value = proj[here, :]
        high, low = split(value)
        right_hi[here, :] = high
        right_lo[here, :] = low
        high, low = split(value.T)
        left_hi[:, here] = high
        left_lo[:, here] = low

    high, low = split(proj[1024:ROWS, :])
    right_hi[1024:ROWS, :] = high
    right_lo[1024:ROWS, :] = low

    def half_gram(half, g):
        rows = pl.ds(pl.multiple_of(256 * half, 256), 256)
        there = slice(32 * g, 32 * g + 1024)
        total = dot(left_hi[rows, :], right_hi[there, :])
        total += dot(left_lo[rows, :], right_hi[there, :])
        total += dot(left_hi[rows, :], right_lo[there, :])
        return total


    def core_sum(g):
        return remote(gram_out.at[g], gram_in.at[g], cs_s.at[g], cs_r.at[g], device(x, y, z, 1 - core))

    def to_plane(g, d):
        tx = around(x, lax.div(d, 4), 4)
        ty = around(y, lax.rem(d, 4), 4)
        src = gram.at[g, pl.ds(pl.multiple_of(64 * ty + 16 * tx, 16), 16), :]
        slot = 15 * g + d - 1
        return remote(src, plane.at[g, x, y], pl_s.at[slot], pl_r.at[slot], device(tx, ty, z, core))

    def give_half(g):
        gram_out[g] = half_gram(1 - core, g)
        core_sum(g).start()
        drains.append(lambda: core_sum(g).wait_send())

    def give_plane(g):
        core_sum(g).wait_recv()
        gram[g] += gram_in[g]

        @pl.loop(1, 16)
        def _(d):
            to_plane(g, d).start()

        plane[g, x, y] = gram[g, pl.ds(pl.multiple_of(64 * y + 16 * x, 16), 16), :]
        loop_drain(functools.partial(to_plane, g), 16)

    give_half(0)
    gram[0] = half_gram(core, 0)
    give_half(1)
    give_plane(0)
    gram[1] = half_gram(core, 1)
    give_plane(1)

    def tile(t):
        return (slice(8 * (t // 4), 8 * (t // 4) + 8), slice(128 * (t % 4), 128 * (t % 4) + 128))

    def scatter(d):
        to = around(z, d, NZ)
        return remote(tiles_out.at[to], tiles_in.at[z], e1_s.at[d - 1], e1_r.at[d - 1], device(x, y, to, core))

    def bring_back(d):
        to = around(z, d, NZ)
        return remote(before_out.at[to], before_in.at[z], e2_s.at[d - 1], e2_r.at[d - 1], device(x, y, to, core))

    def owners(g, act):
        @pl.loop(0, NZ // 2)
        def _(t):
            d = lax.rem(2 * t + g - z + NZ, NZ)

            @pl.when(d > 0)
            def _():
                act(d)

    def give_tiles(g):
        @pl.loop(1, 16)
        def _(d):
            to_plane(g, d).wait_recv()

        state = None
        for i in range(4):
            term = (plane[g, i, 0] + plane[g, i, 1]) + (plane[g, i, 2] + plane[g, i, 3])
            state = term if state is None else state + term
            states[i, g] = state
        for t in range(NZ // 2):
            tiles_out[2 * t + g] = states[(3, g) + tile(t)]
        owners(g, lambda d: scatter(d).start())

    def give_before(g):
        @pl.when(lax.rem(z, 2) == g)
        def _():
            tiles_in[z] = tiles_out[z]

            @pl.loop(1, NZ)
            def _(d):
                scatter(d).wait_recv()

            running = jnp.zeros((8, 128), F32)
            for t in range(NZ):
                before_out[t] = running
                running = running + tiles_in[t]

            @pl.loop(1, NZ)
            def _(d):
                bring_back(d).start()

            before_in[z] = before_out[z]

    own_rows = pl.ds(pl.multiple_of(16 * x, 16), 16)

    def to_owner(i, g):
        to = device(2 * (i // 2) + core, y, z, i % 2)
        here = out.at[0, g, own_rows, :]
        return remote(final.at[i, g], here, f_s.at[4 * g + i], f_r.at[4 * g + x], to)

    def mine(i):
        return jnp.logical_and(x == 2 * (i // 2) + core, core == i % 2)

    def give_means(g):
        def arrived(d):
            bring_back(NZ - d).wait_recv()

        owners(g, arrived)
        for i in range(4):
            count = ((4 * z + i + 1) * (LAG_DEV * P_SIZE)).astype(F32)
            for t in range(NZ // 2):
                final[(i, g) + tile(t)] = (before_in[2 * t + g] + states[(i, g) + tile(t)]) / count

            @pl.when(mine(i))
            def _():
                out[0, g, own_rows, :] = final[i, g]

            @pl.when(jnp.logical_not(mine(i)))
            def _():
                to_owner(i, g).start()

            when_drain(jnp.logical_not(mine(i)), functools.partial(to_owner, i, g))

    def take_means(g):
        for i in range(4):
            @pl.when(jnp.logical_not(jnp.logical_and(x == i, core == x_lo)))
            def _():
                here = out.at[0, g, pl.ds(16 * i, 16), :]
                at = 4 * g + i
                remote(final.at[0, g], here, f_s.at[at], f_r.at[at], device(x, y, z, 1 - core)).wait_recv()

    for act in (give_tiles, give_before, give_means, take_means):
        for g in (0, 1):
            act(g)

    def sent_along_z():
        @pl.loop(1, NZ)
        def _(d):
            scatter(d).wait_send()

    def sent_back():
        @pl.loop(1, NZ)
        def _(d):
            bring_back(d).wait_send()

    drains += [sent_along_z, sent_back]

    for act in drains:
        act()


def body(markov, basis):
    vmem = pl.BlockSpec(memory_space=pltpu.VMEM)
    hbm = pl.BlockSpec(memory_space=pltpu.HBM)
    counts = [2, 2, 15, 15, 24, 24, 24, 24, 8, 8, 2, 2, 30, 30, 15, 15, 15, 15, 8, 8, 2]
    return pl.pallas_call(
        kernel,
        out_shape=jax.ShapeDtypeStruct((1, 2, 64, 512), F32),
        in_specs=[hbm, hbm],
        out_specs=vmem,
        scratch_shapes=[
            pltpu.VMEM((32, 32, 64), F32),
            pltpu.VMEM((16, 32, 128), F32),
            pltpu.VMEM((2, 16, 32, 128), F32),
            pltpu.VMEM((2080, 768), BF16),
            pltpu.VMEM((16, 2, 2, 4, 8, 512), F32),
            pltpu.VMEM((768, 512), BF16),
            pltpu.VMEM((ROWS, 512), F32),
            pltpu.VMEM((ROWS, 512), BF16),
            pltpu.VMEM((ROWS, 512), BF16),
            pltpu.VMEM((512, 1024), BF16),
            pltpu.VMEM((512, 1024), BF16),
            pltpu.VMEM((2, 256, 512), F32),
            pltpu.VMEM((2, 256, 512), F32),
            pltpu.VMEM((2, 256, 512), F32),
            pltpu.VMEM((2, 4, 4, 16, 512), F32),
            pltpu.VMEM((4, 2, 16, 512), F32),
            pltpu.VMEM((NZ, 8, 128), F32),
            pltpu.VMEM((NZ, 8, 128), F32),
            pltpu.VMEM((NZ, 8, 128), F32),
            pltpu.VMEM((NZ, 8, 128), F32),
            pltpu.VMEM((4, 2, 16, 512), F32),
        ]
        + [pltpu.SemaphoreType.DMA((n,)) for n in counts],
        compiler_params=pltpu.CompilerParams(
            collective_id=0, has_side_effects=True, vmem_limit_bytes=62 * 1024 * 1024
        ),
        cost_estimate=pl.CostEstimate(flops=10_000_000_000, bytes_accessed=1_000_000, transcendentals=0),
    )(markov, basis)


def solution(mesh):
    placed = (P("lag", "out", None), P("lag", None))
    return jax.shard_map(
        body, mesh=mesh, in_specs=placed, out_specs=P("lag", None, "out", None), check_vma=False
    )
```

time: 106 us -> 91.4 us (0.86)
  Pallas kernels: 103 us -> 89.6 us
    pallas_call x1, Pallas kernels: 103 us -> 89.6 us  [body(): pl.pallas_call(kernel, out_shape=jax.ShapeDtypeStruct((1, 2, 64, 512), F3...]
    unnamed x5 -> x1, local copies, waits for them, and re-layouts: 2.59 us -> 1.67 us
where the time goes in v2:
time: 91.4 us; the launch traced here: 91.3 us
  Pallas kernels  89.6 us (98%)
  local copies, waits for them, and re-layouts  1.67 us (2%)
    pallas_call x1, Pallas kernels, body(): pl.pallas_call(kernel, out_shape=jax.ShapeDtypeStruct((1, 2, 64, 512), F3...  89.6 us

profile of v2, /device:TPU:1, one launch (start us, length us, event | category | flops | bytes accessed | tf_op | source)
XLA Modules:
  0.0 91.3 jit_solution(15699650108988696131)
XLA Ops:
  0.0 89.6 %shard_map.28 = f32[1,2,64,512]{3,2,1,0:T(8,128)} custom-call(f32[32,32,64]{2,1,0:T(8,128)} %markov_hbm.1, f32[32,512]{1,0:T(8,128)} %basis.1), custom_call_target="tpu_custom_call" | custom-call | flops 10000000000 | bytes 1000000 | tf_op jit(solution)/shard_map/pallas_call | solution.py:479
  89.6 1.7 %copy.4 = f32[1,2,64,512]{3,2,1,0:T(8,128)} copy(f32[1,2,64,512]{3,2,1,0:T(8,128)} %shard_map.28) | data formatting | bytes 524288

commit v3 on v2

--- a/solution.py
+++ b/solution.py
@@ -15,7 +15,11 @@
 
 NZ = 16
 CHUNKS = 8
-SECOND, THIRD, LAST = 3, 6, 7
+X_LAST = (0, 1, 2, 3, 4, 5, 6, 7)
+ORDER = (
+    "M0", "A0", "M1", "A1", "M2", "A2", "M3", "B0", "A3", "A4", "B1", "B2", "A5", "A6", "B3", "B4", "L0", "A7", "B5", "B6",
+    "C0", "C1", "D0", "C2", "D1", "B7", "C3", "D2", "C4", "D3", "C5", "D4", "C6", "D5", "C7", "D6", "D7",
+)
 ROWS = 1056
 TILE_M = 528
 
@@ -134,24 +138,28 @@
 
     loop_drain(lambda d: level1(d, z), NZ)
 
-    def to_block():
-        return remote(packed, pairs.at[0], mk_s.at[0], mk_r.at[0], device(2 * x_hi + core, y, z, x_lo))
-
-    def to_before():
+    def to_block(i):
+        part = pl.ds(4 * i, 4)
+        to = device(2 * x_hi + core, y, z, x_lo)
+        return remote(packed.at[part], pairs.at[0, part], mk_s.at[0, i], mk_r.at[0, i], to)
+
+    def to_before(i):
+        part = pl.ds(4 * i, 4)
         earlier = lag - 1
         to = device(lax.rem(earlier, 4), y, lax.div(earlier, 4), x_lo)
-        return remote(packed, pairs.at[1], mk_s.at[1], mk_r.at[1], to)
-
-    @pl.when(swapped)
-    def _():
-        to_block().start()
-
-    @pl.when(lag > 0)
-    def _():
-        to_before().start()
-
-    when_drain(swapped, to_block)
-    when_drain(lag > 0, to_before)
+        return remote(packed.at[part], pairs.at[1, part], mk_s.at[1, i], mk_r.at[1, i], to)
+
+    def give_quarter(i):
+        @pl.when(swapped)
+        def _():
+            to_block(i).start()
+
+        @pl.when(lag > 0)
+        def _():
+            to_before(i).start()
+
+        when_drain(swapped, functools.partial(to_block, i))
+        when_drain(lag > 0, functools.partial(to_before, i))
 
     @pl.when(jnp.logical_not(swapped))
     def _():
@@ -181,7 +189,10 @@
     def level2(q, d):
         piece = gathered.at[zs_of(q), x_hi, core, y, :, cols]
         x_next, y_next = device(around(x, d, 4), y, z, core), device(x, around(y, d, 4), z, core)
-        to = tuple(jnp.where(core == 0, b, a) for a, b in zip(x_next, y_next))
+        if q in X_LAST:
+            to = tuple(jnp.where(core == 0, b, a) for a, b in zip(x_next, y_next))
+        else:
+            to = x_next
         slot = 3 * q + d - 1
         return remote(piece, piece, b2_s.at[slot], b2_r.at[slot], to)
 
@@ -195,7 +206,11 @@
             to = device(x, around(y, d, 4), z, core)
         return remote(piece, piece, b3_s.at[slot], b3_r.at[slot], to)
 
-    def by_order(act):
+    def by_order(q, act):
+        if q not in X_LAST:
+            act(False)
+            return
+
         for x_last in (True, False):
             @pl.when((core == 0) == x_last)
             def _():
@@ -217,15 +232,15 @@
             for d in (1, 2, 3):
                 level3(q, d, x_last).wait_send()
 
-        by_order(act)
-        drains.append(lambda: by_order(drain))
+        by_order(q, act)
+        drains.append(lambda: by_order(q, drain))
 
     def wait3_start4(q):
         def act(x_last):
             for d in (1, 2, 3):
                 level3(q, d, x_last).wait_recv()
 
-        by_order(act)
+        by_order(q, act)
         level4(q).start()
         drains.append(lambda: level4(q).wait_send())
 
@@ -240,14 +255,18 @@
 
         drains.append(drain)
 
-    def build_lhs():
+    def build_lhs(_):
+        proj[...] = jnp.zeros_like(proj)
+
         @pl.when(swapped)
         def _():
-            to_block().wait_recv()
+            for i in range(4):
+                to_block(i).wait_recv()
 
         @pl.when(block < 4 * NZ - 1)
         def _():
-            to_before().wait_recv()
+            for i in range(4):
+                to_before(i).wait_recv()
 
         first_half = lax.broadcasted_iota(jnp.int32, (32, 128), 1) < 64
 
@@ -289,18 +308,9 @@
             proj[here, :] += dot(lhs[there, :], weights[...])
 
 
-    proj[...] = jnp.zeros_like(proj)
-    for step in range(CHUNKS + LAST):
-        if step < CHUNKS:
-            wait1_start2(step)
-        if 0 <= step - SECOND < CHUNKS:
-            wait2_start3(step - SECOND)
-        if 0 <= step - THIRD < CHUNKS:
-            wait3_start4(step - THIRD)
-        if step == LAST:
-            build_lhs()
-        if 0 <= step - LAST < CHUNKS:
-            compute(step - LAST)
+    acts = dict(M=give_quarter, L=build_lhs, A=wait1_start2, B=wait2_start3, C=wait3_start4, D=compute)
+    for name in ORDER:
+        acts[name[0]](int(name[1]))
 
 
     @pl.loop(0, 8)
@@ -371,10 +381,14 @@
         to = around(z, d, NZ)
         return remote(before_out.at[to], before_in.at[z], e2_s.at[d - 1], e2_r.at[d - 1], device(x, y, to, core))
 
+    def apart(k):
+        half = lax.div(k + 1, 2)
+        return jnp.where(lax.rem(k, 2) == 1, half, -half)
+
     def owners(g, act):
         @pl.loop(0, NZ // 2)
-        def _(t):
-            d = lax.rem(2 * t + g - z + NZ, NZ)
+        def _(k):
+            d = lax.rem(NZ // 2 - lax.rem(g + z, 2) + 2 * apart(k), NZ)
 
             @pl.when(d > 0)
             def _():
@@ -408,28 +422,29 @@
                 before_out[t] = running
                 running = running + tiles_in[t]
 
-            @pl.loop(1, NZ)
-            def _(d):
-                bring_back(d).start()
+            @pl.loop(0, NZ - 1)
+            def _(k):
+                bring_back(NZ // 2 + apart(k)).start()
 
             before_in[z] = before_out[z]
 
     own_rows = pl.ds(pl.multiple_of(16 * x, 16), 16)
 
     def to_owner(i, g):
-        to = device(2 * (i // 2) + core, y, z, i % 2)
+        to = device(2 * lax.div(i, 2) + core, y, z, lax.rem(i, 2))
         here = out.at[0, g, own_rows, :]
         return remote(final.at[i, g], here, f_s.at[4 * g + i], f_r.at[4 * g + x], to)
 
     def mine(i):
-        return jnp.logical_and(x == 2 * (i // 2) + core, core == i % 2)
+        return jnp.logical_and(x == 2 * lax.div(i, 2) + core, core == lax.rem(i, 2))
 
     def give_means(g):
         def arrived(d):
             bring_back(NZ - d).wait_recv()
 
         owners(g, arrived)
-        for i in range(4):
+        for k in range(4):
+            i = lax.rem(2 * (1 - x_hi) + k, 4)
             count = ((4 * z + i + 1) * (LAG_DEV * P_SIZE)).astype(F32)
             for t in range(NZ // 2):
                 final[(i, g) + tile(t)] = (before_in[2 * t + g] + states[(i, g) + tile(t)]) / count
@@ -475,7 +490,7 @@
 def body(markov, basis):
     vmem = pl.BlockSpec(memory_space=pltpu.VMEM)
     hbm = pl.BlockSpec(memory_space=pltpu.HBM)
-    counts = [2, 2, 15, 15, 24, 24, 24, 24, 8, 8, 2, 2, 30, 30, 15, 15, 15, 15, 8, 8, 2]
+    counts = [15, 15, 24, 24, 24, 24, 8, 8, 2, 2, 30, 30, 15, 15, 15, 15, 8, 8, 2]
     return pl.pallas_call(
         kernel,
         out_shape=jax.ShapeDtypeStruct((1, 2, 64, 512), F32),
@@ -504,6 +519,7 @@
             pltpu.VMEM((NZ, 8, 128), F32),
             pltpu.VMEM((4, 2, 16, 512), F32),
         ]
+        + [pltpu.SemaphoreType.DMA((2, 4))] * 2
         + [pltpu.SemaphoreType.DMA((n,)) for n in counts],
         compiler_params=pltpu.CompilerParams(
             collective_id=0, has_side_effects=True, vmem_limit_bytes=62 * 1024 * 1024

time: 91.4 us -> 89 us (0.974)
  Pallas kernels: 89.6 us -> 87.1 us
    pallas_call x1, Pallas kernels: 89.6 us -> 87.1 us  [body(): pl.pallas_call(kernel, out_shape=jax.ShapeDtypeStruct((1, 2, 64, 512), F3...]
where the time goes in v3:
time: 89 us; the launch traced here: 88.8 us
  Pallas kernels  87.1 us (98%)
  local copies, waits for them, and re-layouts  1.67 us (2%)
    pallas_call x1, Pallas kernels, body(): pl.pallas_call(kernel, out_shape=jax.ShapeDtypeStruct((1, 2, 64, 512), F3...  87.1 us

profile of v3, /device:TPU:1, one launch (start us, length us, event | category | flops | bytes accessed | tf_op | source)
XLA Modules:
  0.0 88.8 jit_solution(14559747408271747793)
XLA Ops:
  0.0 87.1 %shard_map.28 = f32[1,2,64,512]{3,2,1,0:T(8,128)} custom-call(f32[32,32,64]{2,1,0:T(8,128)} %markov_hbm.1, f32[32,512]{1,0:T(8,128)} %basis.1), custom_call_target="tpu_custom_call" | custom-call | flops 10000000000 | bytes 1000000 | tf_op jit(solution)/shard_map/pallas_call | solution.py:494
  87.1 1.7 %copy.4 = f32[1,2,64,512]{3,2,1,0:T(8,128)} copy(f32[1,2,64,512]{3,2,1,0:T(8,128)} %shard_map.28) | data formatting | bytes 524288

commit v4 on v3

--- a/solution.py
+++ b/solution.py
@@ -17,8 +17,8 @@
 CHUNKS = 8
 X_LAST = (0, 1, 2, 3, 4, 5, 6, 7)
 ORDER = (
-    "M0", "A0", "M1", "A1", "M2", "A2", "M3", "B0", "A3", "A4", "B1", "B2", "A5", "A6", "B3", "B4", "L0", "A7", "B5", "B6",
-    "C0", "C1", "D0", "C2", "D1", "B7", "C3", "D2", "C4", "D3", "C5", "D4", "C6", "D5", "C7", "D6", "D7",
+    "M0", "M1", "A0", "M2", "A1", "M3", "A2", "A3", "B0", "A4", "B1", "B2", "A5", "A6", "B3", "B4", "L0", "A7", "B5", "C0",
+    "B6", "C1", "D0", "C2", "D1", "C3", "B7", "D2", "C4", "D3", "C5", "D4", "C6", "D5", "C7", "D6", "D7",
 )
 ROWS = 1056
 TILE_M = 528
@@ -41,8 +41,8 @@
 def kernel(
     markov_hbm, basis, out,
     markov, packed, pairs, lhs, gathered, weights, proj, right_hi, right_lo, left_hi, left_lo,
-    gram_out, gram_in, gram, plane, states, tiles_out, tiles_in, before_out, before_in, final,
-    mk_s, mk_r, b1_s, b1_r, b2_s, b2_r, b3_s, b3_r, b4_s, b4_r, cs_s, cs_r, pl_s, pl_r,
+    gram_out, gram_in, gram, via, plane, states, tiles_out, tiles_in, before_out, before_in, final,
+    mk_s, mk_r, b1_s, b1_r, b2_s, b2_r, b3_s, b3_r, b4_s, b4_r, cs_s, cs_r, via_s, via_r, pl_s, pl_r,
     e1_s, e1_r, e2_s, e2_r, f_s, f_r, in_s,
 ):
     lag = lax.axis_index("lag")
@@ -347,6 +347,23 @@
         slot = 15 * g + d - 1
         return remote(src, plane.at[g, x, y], pl_s.at[slot], pl_r.at[slot], device(tx, ty, z, core))
 
+    def half_rows(ty, half):
+        return pl.ds(pl.multiple_of(64 * ty + 32 * half, 32), 32)
+
+    def to_via(g, half):
+        src = gram.at[g, half_rows(around(y, 2, 4), half), :]
+        to = device(x, around(y, (1, 3)[half], 4), z, core)
+        return remote(src, via.at[g, half], via_s.at[2 * g + half], via_r.at[2 * g + half], to)
+
+    def place(tx, dy):
+        return 4 * lax.rem(tx - x + 4, 4) + dy
+
+    def all_planes(act):
+        for dy in (0, 1, 3):
+            @pl.loop(1 if dy == 0 else 0, 4)
+            def _(k):
+                act(4 * k + dy)
+
     def give_half(g):
         gram_out[g] = half_gram(1 - core, g)
         core_sum(g).start()
@@ -356,12 +373,34 @@
         core_sum(g).wait_recv()
         gram[g] += gram_in[g]
 
-        @pl.loop(1, 16)
-        def _(d):
-            to_plane(g, d).start()
+        for half in (0, 1):
+            to_via(g, half).start()
+
+        @pl.loop(1, 4)
+        def _(k):
+            to_plane(g, 4 * k).start()
+
+        for tx in (2, 3):
+            to_plane(g, place(tx, 1)).start()
+        for tx in (0, 1):
+            to_plane(g, place(tx, 3)).start()
 
         plane[g, x, y] = gram[g, pl.ds(pl.multiple_of(64 * y + 16 * x, 16), 16), :]
-        loop_drain(functools.partial(to_plane, g), 16)
+
+        def drain():
+            for half in (0, 1):
+                to_via(g, half).wait_send()
+
+        drains.append(drain)
+
+    def give_rest(g):
+        for half in (0, 1):
+            dy = (1, 3)[half]
+            to_via(g, half).wait_recv()
+            gram[g, half_rows(around(y, dy, 4), half), :] += via[g, half]
+            for k in (0, 1):
+                to_plane(g, place(2 * half + k, dy)).start()
+        drains.append(lambda: all_planes(lambda d: to_plane(g, d).wait_send()))
 
     give_half(0)
     gram[0] = half_gram(core, 0)
@@ -369,6 +408,8 @@
     give_plane(0)
     gram[1] = half_gram(core, 1)
     give_plane(1)
+    give_rest(0)
+    give_rest(1)
 
     def tile(t):
         return (slice(8 * (t // 4), 8 * (t // 4) + 8), slice(128 * (t % 4), 128 * (t % 4) + 128))
@@ -395,13 +436,10 @@
                 act(d)
 
     def give_tiles(g):
-        @pl.loop(1, 16)
-        def _(d):
-            to_plane(g, d).wait_recv()
-
+        all_planes(lambda d: to_plane(g, d).wait_recv())
         state = None
         for i in range(4):
-            term = (plane[g, i, 0] + plane[g, i, 1]) + (plane[g, i, 2] + plane[g, i, 3])
+            term = plane[g, i, y] + (plane[g, i, around(y, 1, 4)] + plane[g, i, around(y, 3, 4)])
             state = term if state is None else state + term
             states[i, g] = state
         for t in range(NZ // 2):
@@ -490,7 +528,7 @@
 def body(markov, basis):
     vmem = pl.BlockSpec(memory_space=pltpu.VMEM)
     hbm = pl.BlockSpec(memory_space=pltpu.HBM)
-    counts = [15, 15, 24, 24, 24, 24, 8, 8, 2, 2, 30, 30, 15, 15, 15, 15, 8, 8, 2]
+    counts = [15, 15, 24, 24, 24, 24, 8, 8, 2, 2, 4, 4, 30, 30, 15, 15, 15, 15, 8, 8, 2]
     return pl.pallas_call(
         kernel,
         out_shape=jax.ShapeDtypeStruct((1, 2, 64, 512), F32),
@@ -511,6 +549,7 @@
             pltpu.VMEM((2, 256, 512), F32),
             pltpu.VMEM((2, 256, 512), F32),
             pltpu.VMEM((2, 256, 512), F32),
+            pltpu.VMEM((2, 2, 32, 512), F32),
             pltpu.VMEM((2, 4, 4, 16, 512), F32),
             pltpu.VMEM((4, 2, 16, 512), F32),
             pltpu.VMEM((NZ, 8, 128), F32),

time: 89 us -> 87.1 us (0.979)
  Pallas kernels: 87.1 us -> 85.2 us
    pallas_call x1, Pallas kernels: 87.1 us -> 85.2 us  [body(): pl.pallas_call(kernel, out_shape=jax.ShapeDtypeStruct((1, 2, 64, 512), F3...]
where the time goes in v4:
time: 87.1 us; the launch traced here: 86.9 us
  Pallas kernels  85.2 us (98%)
  local copies, waits for them, and re-layouts  1.67 us (2%)
    pallas_call x1, Pallas kernels, body(): pl.pallas_call(kernel, out_shape=jax.ShapeDtypeStruct((1, 2, 64, 512), F3...  85.2 us

profile of v4, /device:TPU:1, one launch (start us, length us, event | category | flops | bytes accessed | tf_op | source)
XLA Modules:
  0.0 86.9 jit_solution(14006886900703028591)
XLA Ops:
  0.0 85.2 %shard_map.28 = f32[1,2,64,512]{3,2,1,0:T(8,128)} custom-call(f32[32,32,64]{2,1,0:T(8,128)} %markov_hbm.1, f32[32,512]{1,0:T(8,128)} %basis.1), custom_call_target="tpu_custom_call" | custom-call | flops 10000000000 | bytes 1000000 | tf_op jit(solution)/shard_map/pallas_call | solution.py:532
  85.3 1.7 %copy.4 = f32[1,2,64,512]{3,2,1,0:T(8,128)} copy(f32[1,2,64,512]{3,2,1,0:T(8,128)} %shard_map.28) | data formatting | bytes 524288

commit v5 on v4

--- a/solution.py
+++ b/solution.py
@@ -505,24 +505,31 @@
                 at = 4 * g + i
                 remote(final.at[0, g], here, f_s.at[at], f_r.at[at], device(x, y, z, 1 - core)).wait_recv()
 
-    for act in (give_tiles, give_before, give_means, take_means):
-        for g in (0, 1):
-            act(g)
-
-    def sent_along_z():
-        @pl.loop(1, NZ)
-        def _(d):
-            scatter(d).wait_send()
-
-    def sent_back():
-        @pl.loop(1, NZ)
-        def _(d):
-            bring_back(d).wait_send()
-
-    drains += [sent_along_z, sent_back]
-
-    for act in drains:
-        act()
+    def wait_sent():
+        for act in drains:
+            act()
+        drains.clear()
+
+    for g in (0, 1):
+        give_tiles(g)
+    wait_sent()
+    for g in (0, 1):
+        give_before(g)
+
+    @pl.loop(1, NZ)
+    def _(d):
+        scatter(d).wait_send()
+
+    for g in (0, 1):
+        give_means(g)
+
+    @pl.loop(1, NZ)
+    def _(d):
+        bring_back(d).wait_send()
+
+    for g in (0, 1):
+        take_means(g)
+    wait_sent()
 
 
 def body(markov, basis):

time: 87.1 us -> 86.6 us (level)
  no operation moved by 1% of the time
where the time goes in v5:
time: 86.6 us; the launch traced here: 86.4 us
  Pallas kernels  84.7 us (98%)
  local copies, waits for them, and re-layouts  1.67 us (2%)
    pallas_call x1, Pallas kernels, body(): pl.pallas_call(kernel, out_shape=jax.ShapeDtypeStruct((1, 2, 64, 512), F3...  84.7 us

profile of v5, /device:TPU:1, one launch (start us, length us, event | category | flops | bytes accessed | tf_op | source)
XLA Modules:
  0.0 86.4 jit_solution(12613956086740613518)
XLA Ops:
  0.0 84.7 %shard_map.28 = f32[1,2,64,512]{3,2,1,0:T(8,128)} custom-call(f32[32,32,64]{2,1,0:T(8,128)} %markov_hbm.1, f32[32,512]{1,0:T(8,128)} %basis.1), custom_call_target="tpu_custom_call" | custom-call | flops 10000000000 | bytes 1000000 | tf_op jit(solution)/shard_map/pallas_call | solution.py:539
  84.7 1.7 %copy.4 = f32[1,2,64,512]{3,2,1,0:T(8,128)} copy(f32[1,2,64,512]{3,2,1,0:T(8,128)} %shard_map.28) | data formatting | bytes 524288

commit v6 on v5

--- a/solution.py
+++ b/solution.py
@@ -21,7 +21,7 @@
     "B6", "C1", "D0", "C2", "D1", "C3", "B7", "D2", "C4", "D3", "C5", "D4", "C6", "D5", "C7", "D6", "D7",
 )
 ROWS = 1056
-TILE_M = 528
+TILE_M = 1056
 
 
 def split(value):

time: 86.6 us -> 86.2 us (level)
  no operation moved by 1% of the time
where the time goes in v6:
time: 86.2 us; the launch traced here: 86 us
  Pallas kernels  84.3 us (98%)
  local copies, waits for them, and re-layouts  1.67 us (2%)
    pallas_call x1, Pallas kernels, body(): pl.pallas_call(kernel, out_shape=jax.ShapeDtypeStruct((1, 2, 64, 512), F3...  84.3 us

profile of v6, /device:TPU:1, one launch (start us, length us, event | category | flops | bytes accessed | tf_op | source)
XLA Modules:
  0.0 86.0 jit_solution(17246982893074220853)
XLA Ops:
  0.0 84.3 %shard_map.28 = f32[1,2,64,512]{3,2,1,0:T(8,128)} custom-call(f32[32,32,64]{2,1,0:T(8,128)} %markov_hbm.1, f32[32,512]{1,0:T(8,128)} %basis.1), custom_call_target="tpu_custom_call" | custom-call | flops 10000000000 | bytes 1000000 | tf_op jit(solution)/shard_map/pallas_call | solution.py:539
  84.3 1.7 %copy.4 = f32[1,2,64,512]{3,2,1,0:T(8,128)} copy(f32[1,2,64,512]{3,2,1,0:T(8,128)} %shard_map.28) | data formatting | bytes 524288
